TPU v7x, 32 devices: a whole 2x2x4 slice. The times are simulated.
32 devices in a mesh: row: 4 (over y, x), col: 8 (over z, core).
Axes of the slice: x: 2, y: 2, z: 4, core: 2. Of those that a mesh axis runs over, the one named last changes fastest.
Arguments:
- distances: float32 [1024, 1024], P('row', 'col'), may hold values from 0.5 to 8
- neighbor_ids: int32 [10, 1024], replicated, may hold values from 0 to 1023
- edge_lengths: float32 [10, 1024], P(None, ('row', 'col')), may hold values from 0.125 to 1
- pivots: int32 [2], replicated, may hold values from 0 to 31
Outputs:
- geodesic: float32 [1024, 1024], P('row', 'col')
All inputs are finite; a program needn't handle non-finite values.
Results may differ from a plain program's by a relative error of at most 0.00002.
Values sent between devices are 32-bit elements; how exact they have to be, the bound alone decides.
A program may use at most 64 MiB of HBM per device.

v0:
```python
import jax
import jax.numpy as jnp
from jax import lax
from jax.sharding import PartitionSpec as P

NEIGHBORS = 10
PIVOT = 32


def broadcast(value, axis, source):
    kept = jnp.where(lax.axis_index(axis) == source, value, 0).astype(value.dtype)
    return lax.psum(kept, axis)


def locate(pivot, rows_here, cols_here):
    base = pivot * PIVOT
    row_root = base // rows_here
    col_root = base // cols_here
    return (row_root, col_root, base - row_root * rows_here, base - col_root * cols_here)


def closure(block):

    def relax_one(t, current):
        column = lax.dynamic_slice_in_dim(current, t, 1, 1)
        row_line = lax.dynamic_slice_in_dim(current, t, 1, 0)
        return jnp.minimum(current, column + row_line)

    return lax.fori_loop(0, block.shape[0], relax_one, block)


def minplus(left, right):
    return jnp.min(left[:, :, None] + right[None, :, :], axis=1)


def apply_panels(matrix, cols_panel, rows_panel):
    rows_here = matrix.shape[0]
    width = cols_panel.shape[0]
    block = min(64, rows_here)
    left = cols_panel.T.reshape(rows_here // block, block, width)
    better = lax.map(lambda piece: minplus(piece, rows_panel), left)
    return jnp.minimum(matrix, better.reshape(rows_here, matrix.shape[1]))


def on_device(distances, neighbor_ids, edge_lengths, pivots):
    rows_here, cols_here = distances.shape
    all_lengths = lax.all_gather(edge_lengths, ("row", "col"), axis=1, tiled=True)
    row_start = lax.axis_index("row") * rows_here
    col_start = lax.axis_index("col") * cols_here
    row_ids = row_start + jnp.arange(rows_here, dtype=jnp.int32)
    col_ids = col_start + jnp.arange(cols_here, dtype=jnp.int32)
    matrix = distances
    for k in range(NEIGHBORS):
        ids_rows = lax.dynamic_slice_in_dim(neighbor_ids[k], row_start, rows_here)
        len_rows = lax.dynamic_slice_in_dim(all_lengths[k], row_start, rows_here)
        ids_cols = lax.dynamic_slice_in_dim(neighbor_ids[k], col_start, cols_here)
        len_cols = lax.dynamic_slice_in_dim(all_lengths[k], col_start, cols_here)
        forward = jnp.where(ids_rows[:, None] == col_ids[None, :], len_rows[:, None], jnp.inf)
        backward = jnp.where(row_ids[:, None] == ids_cols[None, :], len_cols[None, :], jnp.inf)
        matrix = jnp.minimum(matrix, jnp.minimum(forward, backward))
    matrix = jnp.where(row_ids[:, None] == col_ids[None, :], jnp.float32(0.0), matrix)
    for q in range(2):
        row_root, col_root, row_off, col_off = locate(pivots[q], rows_here, cols_here)
        own_rows = lax.dynamic_slice_in_dim(matrix, row_off, PIVOT, 0)
        own_cols = lax.dynamic_slice_in_dim(matrix, col_off, PIVOT, 1).T
        panel_rows = broadcast(own_rows, "row", row_root)
        panel_cols = broadcast(own_cols, "col", col_root)
        corner = lax.dynamic_slice_in_dim(own_rows, col_off, PIVOT, 1)
        corner = broadcast(corner, ("row", "col"), row_root * lax.axis_size("col") + col_root)
        closed = closure(corner)
        matrix = apply_panels(matrix, panel_cols, minplus(closed, panel_rows))
    return matrix


def solution(mesh):
    placed = (P("row", "col"), P(), P(None, ("row", "col")), P())
    return jax.shard_map(
        on_device, mesh=mesh, in_specs=placed, out_specs=P("row", "col"), check_vma=False
    )
```

profile of v0, /device:TPU:0, one launch (start us, length us, event | category | flops | bytes accessed | tf_op | source)
XLA Modules:
  0.0 233.1 jit_solution(7379959571927033514)
XLA Ops:
  0.0 0.7 copy-done.2
  0.7 44.3 %all-gather = f32[32,32,10]{1,2,0:T(8,128)S(1)} all-gather(f32[1,32,10]{1,2,0:T(8,128)S(1)} %bitcast.141), channel_id=1, replica_groups=mesh['row'=4,'col'=8] {'row','col'}, dimensions={0}, use_global_device_ids=true | all-gather | bytes 42240 | tf_op jit(solution)/shard_map/all_gather | solution.py:47
  45.4 0.6 copy-done.1
  46.3 0.8 minimum_select_fusion
  47.1 0.7 fusion.24
  48.5 36.9 %psum.43 = f32[32,32]{1,0:T(8,128)S(1)} all-reduce(f32[32,32]{1,0:T(8,128)S(1)} %dynamic-slice_select_fusion.5), channel_id=1, replica_groups=mesh['row'=4,'col'=8] {'row','col'}, use_global_device_ids=true, to_apply=%region_1.2 | all-reduce | flops 1024 | bytes 8192 | tf_op jit(solution)/shard_map/psum | solution.py:12
  85.4 8.8 %while.46 = (s32[]{:T(128)}, f32[32,32]{1,0:T(8,128)S(1)}, s32[]{:T(128)}) while((s32[]{:T(128)}, f32[32,32]{1,0:T(8,128)S(1)}, s32[]{:T(128)}) %tuple.116), condition=%wide.region_3.4_spmd, body=%wide.region_2.3_spmd.sunk | while | flops 2050 | bytes 9013 | solution.py:29
  85.7 0.2 dynamic-slice_reduce_fusion.4
  85.9 0.2 dynamic-slice_reduce_fusion.4
  86.2 0.2 dynamic-slice_reduce_fusion.4
  86.5 0.2 dynamic-slice_reduce_fusion.4
  86.8 0.2 dynamic-slice_reduce_fusion.4
  94.2 15.9 %psum.44 = f32[32,128]{1,0:T(8,128)S(1)} all-reduce(f32[32,128]{1,0:T(8,128)S(1)} %dynamic-slice_select_fusion.4), channel_id=1, replica_groups=mesh['row'=4,'col'=8] {'row'}, use_global_device_ids=true, to_apply=%region_4.5 | all-reduce | flops 4096 | bytes 32768 | tf_op jit(solution)/shard_map/psum | solution.py:12
  110.0 0.2 add_reduce_fusion.3
  110.4 27.1 %psum.42 = f32[4,64,32]{2,1,0:T(8,128)S(1)} all-reduce(f32[4,64,32]{2,1,0:T(8,128)S(1)} %bitcast.98), channel_id=1, replica_groups=mesh['row'=4,'col'=8] {'col'}, use_global_device_ids=true, to_apply=%region_0.1 | all-reduce | flops 8192 | bytes 65536 | tf_op jit(solution)/shard_map/psum | solution.py:12
  137.4 1.7 while.47
  137.5 0.4 add_reduce_fusion.6
  137.9 0.4 add_reduce_fusion.6
  138.3 0.4 add_reduce_fusion.6
  138.8 0.4 add_reduce_fusion.6
  139.2 0.8 bitcast_minimum_fusion.1
  140.8 36.9 %psum.46 = f32[32,32]{1,0:T(8,128)S(1)} all-reduce(f32[32,32]{1,0:T(8,128)S(1)} %dynamic-slice_select_fusion.3), channel_id=1, replica_groups=mesh['row'=4,'col'=8] {'row','col'}, use_global_device_ids=true, to_apply=%region_10.11 | all-reduce | flops 1024 | bytes 8192 | tf_op jit(solution)/shard_map/psum | solution.py:12
  177.8 8.8 %while.48 = (s32[]{:T(128)}, f32[32,32]{1,0:T(8,128)S(1)}, s32[]{:T(128)}) while((s32[]{:T(128)}, f32[32,32]{1,0:T(8,128)S(1)}, s32[]{:T(128)}) %tuple.122), condition=%wide.region_12.13_spmd, body=%wide.region_11.12_spmd.sunk | while | flops 2050 | bytes 9013 | solution.py:29
  186.5 16.8 %psum.47 = f32[32,128]{1,0:T(8,128)S(1)} all-reduce(f32[32,128]{1,0:T(8,128)S(1)} %dynamic-slice_select_fusion.2), channel_id=1, replica_groups=mesh['row'=4,'col'=8] {'row'}, use_global_device_ids=true, to_apply=%region_13.14 | all-reduce | flops 4096 | bytes 32768 | tf_op jit(solution)/shard_map/psum | solution.py:12
  203.3 0.2 add_reduce_fusion.2
  203.7 27.1 %psum.45 = f32[4,64,32]{2,1,0:T(8,128)S(1)} all-reduce(f32[4,64,32]{2,1,0:T(8,128)S(1)} %bitcast.99), channel_id=1, replica_groups=mesh['row'=4,'col'=8] {'col'}, use_global_device_ids=true, to_apply=%region_9.10 | all-reduce | flops 8192 | bytes 65536 | tf_op jit(solution)/shard_map/psum | solution.py:12
  230.8 1.7 while.49
  230.8 0.4 add_reduce_fusion.7
  231.2 0.4 add_reduce_fusion.7
  231.6 0.4 add_reduce_fusion.7
  232.1 0.4 add_reduce_fusion.7
  232.5 0.7 bitcast_minimum_fusion
  (243 shorter events, 17.1 us)
Async XLA Ops:
  0.0 0.7 copy-start.2
  45.2 0.8 copy-start.1
  45.3 1.0 copy-start
  46.3 0.8 copy-start.3
where the time goes:
time: 234 us; the launch traced here: 233 us
  blocking collectives  205 us (88%)
  local copies, waits for them, and re-layouts  14.9 us (6%)
  other arithmetic  10.8 us (5%)
    psum x6, blocking collectives, broadcast(): return lax.psum(kept, axis)  161 us
    all_gather x1, blocking collectives, on_device(): lax.all_gather(edge_lengths, ('row', 'col'), axis=1, tiled=True)  44.3 us
    dynamic_slice x64, local copies, waits for them, and re-layouts, relax_one(): column = lax.dynamic_slice_in_dim(current, t, 1, 1)  11.6 us
    min x64, other arithmetic, relax_one(): return jnp.minimum(current, column + row_line)  4.73 us

commit v1 on v0

v1 whole, which is shorter than its diff:
```python
import functools

import jax
import jax.numpy as jnp
from jax import lax
from jax.experimental import pallas as pl
from jax.experimental.pallas import tpu as pltpu
from jax.sharding import PartitionSpec as P

NEIGHBORS = 10
PIVOT = 32
MESH = pl.DeviceIdType.MESH


def relax(block, row_ids, col_ids, ids_rows, len_rows, ids_cols, len_cols):
    for k in range(NEIGHBORS):
        forward = jnp.where(ids_rows[:, k : k + 1] == col_ids, len_rows[:, k : k + 1], jnp.inf)
        backward = jnp.where(row_ids == ids_cols[k : k + 1, :], len_cols[k : k + 1, :], jnp.inf)
        block = jnp.minimum(block, jnp.minimum(forward, backward))
    return jnp.where(row_ids == col_ids, jnp.float32(0.0), block)


def minplus(total, left, right):
    for k in range(left.shape[1]):
        term = left[:, k : k + 1] + right[k : k + 1, :]
        total = term if total is None else jnp.minimum(total, term)
    return total


def pick(items, index):
    chosen = items[0]
    index = jnp.full(chosen.shape, index, jnp.int32)
    for i in range(1, len(items)):
        chosen = jnp.where(index == i, items[i], chosen)
    return chosen


def kernel(nr, nc, pivots, dist, ids, lens, out,
           e_send, e_recv, e_all, e_t, c_send, c_recv, c_all, c_full,
           r_recv, k_recv, t_ref,
           es_sem, er_sem, rs_sem, rr_sem, cs_sem, cr_sem,
           ga_s, ga_r, ge_s, ge_r, ks_sem, kr_sem):
    rows_here, cols_here = dist.shape
    width = lens.shape[1]
    half = rows_here // 2
    piece = half // nc
    pair = 2 * PIVOT
    r, c = lax.axis_index("row"), lax.axis_index("col")
    row_peers = [lax.rem(r + i, nr) for i in range(1, nr)]
    col_peers = [lax.rem(c + i, nc) for i in range(1, nc)]

    barrier = pltpu.get_barrier_semaphore()
    for peer in row_peers:
        pl.semaphore_signal(barrier, inc=1, device_id=(peer, c), device_id_type=MESH)
    for peer in col_peers:
        pl.semaphore_signal(barrier, inc=1, device_id=(r, peer), device_id_type=MESH)

    p = [pivots[q] for q in range(2)]
    base = [p[q] * PIVOT for q in range(2)]
    row_root = [lax.div(base[q], rows_here) for q in range(2)]
    col_root = [lax.div(base[q], cols_here) for q in range(2)]
    row_slot = [lax.rem(p[q], rows_here // PIVOT) for q in range(2)]
    col_slot = [lax.rem(p[q], cols_here // PIVOT) for q in range(2)]
    row_cuts = [slice(i, i + PIVOT) for i in range(0, rows_here, PIVOT)]
    col_cuts = [slice(i, i + PIVOT) for i in range(0, cols_here, PIVOT)]

    own_len = lens[...]
    e_send[0:NEIGHBORS, :] = jnp.concatenate([own_len] * nr, axis=1)
    e_send[NEIGHBORS:16, :] = jnp.zeros((16 - NEIGHBORS, cols_here), jnp.float32)
    e_recv[r] = e_send[...]
    for q in range(2):
        r_recv[r, q * PIVOT : (q + 1) * PIVOT, :] = pick([dist[cut, :] for cut in row_cuts], row_slot[q])
    groups = cols_here // PIVOT
    lane = lax.broadcasted_iota(jnp.int32, (1, cols_here), 1)
    source = jnp.where(
        lane // PIVOT % 2 == 0, jnp.full_like(lane, col_slot[0]), jnp.full_like(lane, col_slot[1]))
    turn = (lane // PIVOT - source + groups) % groups
    packed = jnp.zeros((half, cols_here), jnp.float32)
    for h in range(2):
        part = dist[h * half : (h + 1) * half, :]
        for g in range(groups):
            turned = pltpu.roll(part, g * PIVOT, 1) if g else part
            packed = jnp.where((turn == g) & (lane // pair == h), turned, packed)
    for j in range(nc):
        c_send[j] = packed[j * piece : (j + 1) * piece, :]
    c_recv[c] = c_send[c]

    pl.semaphore_wait(barrier, nr + nc - 2)

    def send(src, dst, send_sem, recv_sem, peer):
        copy = pltpu.make_async_remote_copy(
            src_ref=src, dst_ref=dst, send_sem=send_sem, recv_sem=recv_sem,
            device_id=peer, device_id_type=MESH)
        copy.start()
        return copy

    def arrive(slot, sem, peer):
        pltpu.make_async_remote_copy(
            src_ref=slot, dst_ref=slot, send_sem=sem, recv_sem=sem,
            device_id=peer, device_id_type=MESH).wait_recv()

    sent = []
    for i, peer in enumerate(col_peers):
        sent.append(send(c_send.at[peer], c_recv.at[c], cs_sem.at[i], cr_sem.at[c], (r, peer)))
    for i, peer in enumerate(row_peers):
        sent.append(send(e_send, e_recv.at[r], es_sem.at[i], er_sem.at[r], (peer, c)))
    for i, peer in enumerate(row_peers):
        sent.append(send(r_recv.at[r], r_recv.at[r], rs_sem.at[i], rr_sem.at[r], (peer, c)))

    ids_rows = []
    for t in range(rows_here // cols_here):
        start = pl.multiple_of(r * rows_here + t * cols_here, cols_here)
        ids_rows.append(ids[:, pl.ds(start, cols_here)].T)
    ids_rows = jnp.concatenate(ids_rows, axis=0)
    ids_cols = ids[:, pl.ds(pl.multiple_of(c * cols_here, cols_here), cols_here)]
    ids_p = []
    id_tiles = [ids[:, j * cols_here : (j + 1) * cols_here] for j in range(nc)]
    for q in range(2):
        turned = pick(id_tiles, col_root[q]).T
        ids_p.append(pick([turned[cut, :] for cut in col_cuts], col_slot[q]))
    ids_p = jnp.concatenate(ids_p, axis=0)

    for peer in row_peers:
        arrive(e_recv.at[peer], er_sem.at[peer], (peer, c))
    lane_e = lax.broadcasted_iota(jnp.int32, (16, cols_here), 1)
    edges = e_recv[0]
    for i in range(1, nr):
        edges = jnp.where(lane_e // width == i, e_recv[i], edges)
    e_all[c] = edges
    for i, peer in enumerate(col_peers):
        sent.append(send(e_all.at[c], e_all.at[c], ge_s.at[i], ge_r.at[c], (r, peer)))
    for peer in col_peers:
        arrive(c_recv.at[peer], cr_sem.at[peer], (r, peer))
    lane_c = lax.broadcasted_iota(jnp.int32, (piece, cols_here), 1)
    c_all[c] = jnp.where(lane_c % pair < PIVOT,
                         pick([c_recv[j] for j in range(nc)], col_root[0]),
                         pick([c_recv[j] for j in range(nc)], col_root[1]))
    for i, peer in enumerate(col_peers):
        sent.append(send(c_all.at[c], c_all.at[c], ga_s.at[i], ga_r.at[c], (r, peer)))

    for peer in col_peers:
        arrive(c_all.at[peer], ga_r.at[peer], (r, peer))
    cols_packed = jnp.concatenate([c_all[j] for j in range(nc)], axis=0)
    c_full[0:half, :] = cols_packed
    c_full[half:rows_here, :] = pltpu.roll(cols_packed, pair, 1)
    cuts = [c_full[cut, :] for cut in row_cuts]
    first = pick(cuts, row_slot[0])
    second = pltpu.roll(pick(cuts, row_slot[1]), pair, 1)
    lane_k = lax.broadcasted_iota(jnp.int32, (PIVOT, cols_here), 1)
    k_recv[r] = jnp.where(lane_k < pair, first, second)
    for i, peer in enumerate(row_peers):
        sent.append(send(k_recv.at[r], k_recv.at[r], ks_sem.at[i], kr_sem.at[r], (peer, c)))

    for peer in col_peers:
        arrive(e_all.at[peer], ge_r.at[peer], (r, peer))
    for j in range(nc):
        e_t[j] = e_all[j].T

    def lengths_of(index):
        start = pl.multiple_of(index // nc * width, width)
        return e_t[index % nc, pl.ds(start, width), :]

    len_rows = jnp.concatenate([lengths_of(r * nc + j) for j in range(nc)], axis=0)
    len_cols = jnp.concatenate([lengths_of(c * nr + j) for j in range(nr)], axis=0).T
    steps = PIVOT // width
    len_p = []
    tiles = [e_all[j] for j in range(nc)]
    for index in [p[q] * steps + j for q in range(2) for j in range(steps)]:
        turned = pick(tiles, lax.rem(index, nc)).T
        len_p.append(pick([turned[i * width : (i + 1) * width, :] for i in range(nr)],
                          lax.div(index, nc)))
    len_p = jnp.concatenate(len_p, axis=0)
    ids_p_cols = ids_p.T
    len_p_cols = len_p.T

    row_ids = r * rows_here + lax.broadcasted_iota(jnp.int32, (rows_here, 1), 0)
    col_ids = c * cols_here + lax.broadcasted_iota(jnp.int32, (1, cols_here), 1)
    at_s = lax.broadcasted_iota(jnp.int32, (pair, 1), 0)
    p_rows = jnp.where(at_s < PIVOT, base[0] + at_s, base[1] + at_s - PIVOT)
    at_l = lax.broadcasted_iota(jnp.int32, (1, pair), 1)
    p_cols = jnp.where(at_l < PIVOT, base[0] + at_l, base[1] + at_l - PIVOT)

    for peer in row_peers:
        arrive(r_recv.at[peer], rr_sem.at[peer], (peer, c))
    rows_panel = jnp.concatenate(
        [pick([r_recv[i, q * PIVOT : (q + 1) * PIVOT, :] for i in range(nr)], row_root[q])
         for q in range(2)], axis=0)
    rows_panel = relax(rows_panel, p_rows, col_ids, ids_p, len_p, ids_cols, len_cols)
    out[...] = relax(dist[...], row_ids, col_ids, ids_rows, len_rows, ids_cols, len_cols)
    c_full[:, 0:pair] = relax(
        c_full[:, 0:pair], row_ids, p_cols, ids_rows, len_rows, ids_p_cols, len_p_cols)

    for peer in row_peers:
        arrive(k_recv.at[peer], kr_sem.at[peer], (peer, c))
    corner = jnp.concatenate(
        [pick([k_recv[i] for i in range(nr)], row_root[q])[:, q * pair : (q + 1) * pair]
         for q in range(2)], axis=0)
    corner = relax(corner, p_rows, p_cols, ids_p, len_p, ids_p_cols, len_p_cols)
    corner = lax.fori_loop(0, 6, lambda _, a: minplus(None, a, a), corner)
    t_ref[...] = minplus(None, corner, rows_panel)

    def finish(b, carry):
        at = pl.ds(pl.multiple_of(b * PIVOT, PIVOT), PIVOT)
        out[at, :] = minplus(out[at, :], c_full[at, 0:pair], t_ref[...])
        return carry

    lax.fori_loop(0, rows_here // PIVOT, finish, 0)
    for copy in sent:
        copy.wait_send()


def on_device(nr, nc, distances, neighbor_ids, edge_lengths, pivots):
    rows_here, cols_here = distances.shape
    half = rows_here // 2
    piece = half // nc
    vmem = pl.BlockSpec(memory_space=pltpu.VMEM)
    f32 = jnp.float32
    dma = pltpu.SemaphoreType.DMA
    return pl.pallas_call(
        functools.partial(kernel, nr, nc),
        out_shape=jax.ShapeDtypeStruct(distances.shape, f32),
        in_specs=[pl.BlockSpec(memory_space=pltpu.SMEM), vmem, vmem, vmem],
        out_specs=vmem,
        scratch_shapes=[
            pltpu.VMEM((16, cols_here), f32),
            pltpu.VMEM((nr, 16, cols_here), f32),
            pltpu.VMEM((nc, 16, cols_here), f32),
            pltpu.VMEM((nc, cols_here, 16), f32),
            pltpu.VMEM((nc, piece, cols_here), f32),
            pltpu.VMEM((nc, piece, cols_here), f32),
            pltpu.VMEM((nc, piece, cols_here), f32),
            pltpu.VMEM((rows_here, cols_here), f32),
            pltpu.VMEM((nr, 2 * PIVOT, cols_here), f32),
            pltpu.VMEM((nr, PIVOT, cols_here), f32),
            pltpu.VMEM((2 * PIVOT, cols_here), f32),
            dma((nr,)), dma((nr,)), dma((nr,)), dma((nr,)), dma((nc,)), dma((nc,)),
            dma((nc,)), dma((nc,)), dma((nc,)), dma((nc,)), dma((nr,)), dma((nr,)),
        ],
        compiler_params=pltpu.CompilerParams(
            collective_id=0, has_side_effects=True, vmem_limit_bytes=32 * 1024 * 1024),
    )(pivots, distances, neighbor_ids, edge_lengths)


def solution(mesh):
    placed = (P("row", "col"), P(), P(None, ("row", "col")), P())
    body = functools.partial(on_device, mesh.shape["row"], mesh.shape["col"])
    return jax.shard_map(
        body, mesh=mesh, in_specs=placed, out_specs=P("row", "col"), check_vma=False
    )
```

time: 234 us -> 30.7 us (0.13)
  blocking collectives: 205 us -> 0 us
  Pallas kernels: 0 us -> 26.7 us
  local copies, waits for them, and re-layouts: 14.9 us -> 3.75 us
  other arithmetic: 10.8 us -> 0 us
    psum x6 -> x0, blocking collectives: 161 us -> none  [broadcast(): return lax.psum(kept, axis)]
    all_gather x1 -> x0, blocking collectives: 44.3 us -> none  [on_device(): lax.all_gather(edge_lengths, ('row', 'col'), axis=1, tiled=True)]
    pallas_call x0 -> x1, Pallas kernels: none -> 26.7 us  [on_device(): pl.pallas_call(functools.partial(kernel, nr, nc), out_shape=jax.ShapeDtyp...]
    dynamic_slice x74 -> x0, local copies, waits for them, and re-layouts: 11.7 us -> none  [the longest x64 11.6 us: relax_one(): column = lax.dynamic_slice_in_dim(current, t, 1, 1)]
    min x66 -> x0, other arithmetic: 6.24 us -> none  [the longest x64 4.73 us: relax_one(): return jnp.minimum(current, column + row_line)]
    reduce_min x10 -> x0, other arithmetic: 3.37 us -> none  [minplus(): return jnp.min(left[:, :, None] + right[None, :, :], axis=1)]
where the time goes in v1:
time: 30.7 us; the launch traced here: 30.4 us
  Pallas kernels  26.7 us (87%)
  local copies, waits for them, and re-layouts  3.75 us (12%)
    pallas_call x1, Pallas kernels, on_device(): pl.pallas_call(functools.partial(kernel, nr, nc), out_shape=jax.ShapeDtyp...  26.7 us
    unnamed x9, local copies, waits for them, and re-layouts  3.75 us

profile of v1, /device:TPU:0, one launch (start us, length us, event | category | flops | bytes accessed | tf_op | source)
XLA Modules:
  0.0 30.4 jit_solution(16348363051246657936)
XLA Ops:
  0.0 0.0 copy-start
  0.0 0.9 %copy-done = f32[256,128]{1,0:T(8,128)S(1)} copy-done((f32[256,128]{1,0:T(8,128)S(1)}, f32[256,128]{1,0:T(8,128)}, u32[]{:S(2)}) %copy-start) | copy-done | bytes 131096
  0.9 0.0 copy-start.1
  0.9 0.8 %copy-done.1 = s32[10,1024]{1,0:T(8,128)S(1)} copy-done((s32[10,1024]{1,0:T(8,128)S(1)}, s32[10,1024]{1,0:T(8,128)}, u32[]{:S(2)}) %copy-start.1) | copy-done | bytes 40984
  1.7 0.0 copy-start.2
  1.7 0.7 %copy-done.2 = f32[10,32]{1,0:T(8,128)S(1)} copy-done((f32[10,32]{1,0:T(8,128)S(1)}, f32[10,32]{1,0:T(8,128)}, u32[]{:S(2)}) %copy-start.2) | copy-done | bytes 1304
  2.4 0.0 copy-start.3
  2.4 0.7 %copy-done.3 = s32[2]{0:T(128)S(1)} copy-done((s32[2]{0:T(128)S(1)}, s32[2]{0:T(128)}, u32[]{:S(2)}) %copy-start.3) | copy-done | bytes 32
  3.1 26.7 %shard_map.46 = f32[256,128]{1,0:T(8,128)S(1)} custom-call(s32[2]{0:T(128)S(1)} %copy-done.3, f32[256,128]{1,0:T(8,128)S(1)} %copy-done, s32[10,1024]{1,0:T(8,128)S(1)} %copy-done.1, f32[10,32]{1,0:T(8,128)S(1)} %copy-done.2), custom_call_target="tpu_custom_call" | custom-call | tf_op jit(solution)/shard_map/pallas_call | solution.py:219
  29.8 0.7 %copy.6 = f32[256,128]{1,0:T(8,128)} copy(f32[256,128]{1,0:T(8,128)S(1)} %shard_map.46) | data formatting | bytes 262144
Async XLA Ops:
  0.0 0.9 %copy-start = (f32[256,128]{1,0:T(8,128)S(1)}, f32[256,128]{1,0:T(8,128)}, u32[]{:S(2)}) copy-start(f32[256,128]{1,0:T(8,128)} %dist.1) | copy-start | bytes 393220
  0.9 0.8 %copy-start.1 = (s32[10,1024]{1,0:T(8,128)S(1)}, s32[10,1024]{1,0:T(8,128)}, u32[]{:S(2)}) copy-start(s32[10,1024]{1,0:T(8,128)} %ids.1) | copy-start | bytes 122884
  1.7 0.7 %copy-start.2 = (f32[10,32]{1,0:T(8,128)S(1)}, f32[10,32]{1,0:T(8,128)}, u32[]{:S(2)}) copy-start(f32[10,32]{1,0:T(8,128)} %lens.1) | copy-start | bytes 3844
  2.4 0.7 %copy-start.3 = (s32[2]{0:T(128)S(1)}, s32[2]{0:T(128)}, u32[]{:S(2)}) copy-start(s32[2]{0:T(128)} %pivots.1) | copy-start | bytes 28

commit v2 on v1

--- a/solution.py
+++ b/solution.py
@@ -35,7 +35,7 @@
     return chosen
 
 
-def kernel(nr, nc, pivots, dist, ids, lens, out,
+def kernel(nr, nc, pivots_in, dist_in, ids_in, lens_in, out, pivots, dist, ids, lens, in_sem,
            e_send, e_recv, e_all, e_t, c_send, c_recv, c_all, c_full,
            r_recv, k_recv, t_ref,
            es_sem, er_sem, rs_sem, rr_sem, cs_sem, cr_sem,
@@ -49,12 +49,22 @@
     row_peers = [lax.rem(r + i, nr) for i in range(1, nr)]
     col_peers = [lax.rem(c + i, nc) for i in range(1, nc)]
 
+    loads = [
+        pltpu.make_async_copy(src, dst, in_sem.at[i])
+        for i, (src, dst) in enumerate(
+            [(pivots_in, pivots), (dist_in, dist), (lens_in, lens), (ids_in, ids)])
+    ]
+    for load in loads:
+        load.start()
+
     barrier = pltpu.get_barrier_semaphore()
     for peer in row_peers:
         pl.semaphore_signal(barrier, inc=1, device_id=(peer, c), device_id_type=MESH)
     for peer in col_peers:
         pl.semaphore_signal(barrier, inc=1, device_id=(r, peer), device_id_type=MESH)
 
+    for load in loads:
+        load.wait()
     p = [pivots[q] for q in range(2)]
     base = [p[q] * PIVOT for q in range(2)]
     row_root = [lax.div(base[q], rows_here) for q in range(2)]
@@ -219,9 +229,14 @@
     return pl.pallas_call(
         functools.partial(kernel, nr, nc),
         out_shape=jax.ShapeDtypeStruct(distances.shape, f32),
-        in_specs=[pl.BlockSpec(memory_space=pltpu.SMEM), vmem, vmem, vmem],
+        in_specs=[pl.BlockSpec(memory_space=pltpu.HBM)] * 4,
         out_specs=vmem,
         scratch_shapes=[
+            pltpu.SMEM(pivots.shape, jnp.int32),
+            pltpu.VMEM(distances.shape, f32),
+            pltpu.VMEM(neighbor_ids.shape, jnp.int32),
+            pltpu.VMEM(edge_lengths.shape, f32),
+            dma((4,)),
             pltpu.VMEM((16, cols_here), f32),
             pltpu.VMEM((nr, 16, cols_here), f32),
             pltpu.VMEM((nc, 16, cols_here), f32),

time: 30.7 us -> 30.4 us (level)
  no operation moved by 1% of the time
where the time goes in v2:
time: 30.4 us; the launch traced here: 30.1 us
  Pallas kernels  26.4 us (87%)
  local copies, waits for them, and re-layouts  3.75 us (12%)
    pallas_call x1, Pallas kernels, on_device(): pl.pallas_call(functools.partial(kernel, nr, nc), out_shape=jax.ShapeDtyp...  26.4 us
    unnamed x9, local copies, waits for them, and re-layouts  3.75 us

profile of v2, /device:TPU:0, one launch (start us, length us, event | category | flops | bytes accessed | tf_op | source)
XLA Modules:
  0.0 30.1 jit_solution(3273219529442729908)
XLA Ops:
  0.0 0.0 copy-start
  0.0 0.9 %copy-done = f32[256,128]{1,0:T(8,128)S(1)} copy-done((f32[256,128]{1,0:T(8,128)S(1)}, f32[256,128]{1,0:T(8,128)}, u32[]{:S(2)}) %copy-start) | copy-done | bytes 131096
  0.9 0.0 copy-start.1
  0.9 0.8 %copy-done.1 = s32[10,1024]{1,0:T(8,128)S(1)} copy-done((s32[10,1024]{1,0:T(8,128)S(1)}, s32[10,1024]{1,0:T(8,128)}, u32[]{:S(2)}) %copy-start.1) | copy-done | bytes 40984
  1.7 0.0 copy-start.2
  1.7 0.7 %copy-done.2 = f32[10,32]{1,0:T(8,128)S(1)} copy-done((f32[10,32]{1,0:T(8,128)S(1)}, f32[10,32]{1,0:T(8,128)}, u32[]{:S(2)}) %copy-start.2) | copy-done | bytes 1304
  2.4 0.0 copy-start.3
  2.4 0.7 %copy-done.3 = s32[2]{0:T(128)S(1)} copy-done((s32[2]{0:T(128)S(1)}, s32[2]{0:T(128)}, u32[]{:S(2)}) %copy-start.3) | copy-done | bytes 32
  3.1 26.4 %shard_map.46 = f32[256,128]{1,0:T(8,128)S(1)} custom-call(s32[2]{0:T(128)S(1)} %copy-done.3, f32[256,128]{1,0:T(8,128)S(1)} %copy-done, s32[10,1024]{1,0:T(8,128)S(1)} %copy-done.1, f32[10,32]{1,0:T(8,128)S(1)} %copy-done.2), custom_call_target="tpu_custom_call" | custom-call | tf_op jit(solution)/shard_map/pallas_call | solution.py:229
  29.5 0.7 %copy.6 = f32[256,128]{1,0:T(8,128)} copy(f32[256,128]{1,0:T(8,128)S(1)} %shard_map.46) | data formatting | bytes 262144
Async XLA Ops:
  0.0 0.9 %copy-start = (f32[256,128]{1,0:T(8,128)S(1)}, f32[256,128]{1,0:T(8,128)}, u32[]{:S(2)}) copy-start(f32[256,128]{1,0:T(8,128)} %dist_in.1) | copy-start | bytes 393220
  0.9 0.8 %copy-start.1 = (s32[10,1024]{1,0:T(8,128)S(1)}, s32[10,1024]{1,0:T(8,128)}, u32[]{:S(2)}) copy-start(s32[10,1024]{1,0:T(8,128)} %ids_in.1) | copy-start | bytes 122884
  1.7 0.7 %copy-start.2 = (f32[10,32]{1,0:T(8,128)S(1)}, f32[10,32]{1,0:T(8,128)}, u32[]{:S(2)}) copy-start(f32[10,32]{1,0:T(8,128)} %lens_in.1) | copy-start | bytes 3844
  2.4 0.7 %copy-start.3 = (s32[2]{0:T(128)S(1)}, s32[2]{0:T(128)}, u32[]{:S(2)}) copy-start(s32[2]{0:T(128)} %pivots_in.1) | copy-start | bytes 28

commit v3 on v2

--- a/solution.py
+++ b/solution.py
@@ -252,7 +252,7 @@
             dma((nc,)), dma((nc,)), dma((nc,)), dma((nc,)), dma((nr,)), dma((nr,)),
         ],
         compiler_params=pltpu.CompilerParams(
-            collective_id=0, has_side_effects=True, vmem_limit_bytes=32 * 1024 * 1024),
+            collective_id=0, has_side_effects=True, vmem_limit_bytes=60 * 1024 * 1024),
     )(pivots, distances, neighbor_ids, edge_lengths)
 
 

time: 30.4 us -> 28.6 us (0.941)
  local copies, waits for them, and re-layouts: 3.75 us -> 1.57 us
  Pallas kernels: 26.4 us -> 26.8 us
    unnamed x9 -> x1, local copies, waits for them, and re-layouts: 3.75 us -> 1.57 us
    pallas_call x1, Pallas kernels: 26.4 us -> 26.8 us  [on_device(): pl.pallas_call(functools.partial(kernel, nr, nc), out_shape=jax.ShapeDtyp...]
where the time goes in v3:
time: 28.6 us; the launch traced here: 28.4 us
  Pallas kernels  26.8 us (94%)
  local copies, waits for them, and re-layouts  1.57 us (5%)
    pallas_call x1, Pallas kernels, on_device(): pl.pallas_call(functools.partial(kernel, nr, nc), out_shape=jax.ShapeDtyp...  26.8 us
    unnamed x1, local copies, waits for them, and re-layouts  1.57 us

profile of v3, /device:TPU:0, one launch (start us, length us, event | category | flops | bytes accessed | tf_op | source)
XLA Modules:
  0.0 28.4 jit_solution(8816179805025001621)
XLA Ops:
  0.0 26.8 %shard_map.46 = f32[256,128]{1,0:T(8,128)} custom-call(s32[2]{0:T(128)} %pivots_in.1, f32[256,128]{1,0:T(8,128)} %dist_in.1, s32[10,1024]{1,0:T(8,128)} %ids_in.1, f32[10,32]{1,0:T(8,128)} %lens_in.1), custom_call_target="tpu_custom_call" | custom-call | tf_op jit(solution)/shard_map/pallas_call | solution.py:229
  26.8 1.6 %copy.6 = f32[256,128]{1,0:T(8,128)} copy(f32[256,128]{1,0:T(8,128)} %shard_map.46) | data formatting | bytes 262144

commit v4 on v3

v4 whole, which is shorter than its diff:
```python
import functools

import jax
import jax.numpy as jnp
from jax import lax
from jax.experimental import pallas as pl
from jax.experimental.pallas import tpu as pltpu
from jax.sharding import PartitionSpec as P

NEIGHBORS = 10
PIVOT = 32
MESH = pl.DeviceIdType.MESH


def edge_bound(row_ids, col_ids, ids_rows, len_rows, ids_cols, len_cols):
    bound = jnp.where(row_ids == col_ids, jnp.float32(0.0), jnp.inf)
    for k in range(NEIGHBORS):
        forward = jnp.where(ids_rows[:, k : k + 1] == col_ids, len_rows[:, k : k + 1], jnp.inf)
        backward = jnp.where(row_ids == ids_cols[k : k + 1, :], len_cols[k : k + 1, :], jnp.inf)
        bound = jnp.minimum(bound, jnp.minimum(forward, backward))
    return bound


def minplus(total, left, right):
    for k in range(left.shape[1]):
        term = left[:, k : k + 1] + right[k : k + 1, :]
        total = term if total is None else jnp.minimum(total, term)
    return total


def pick(items, index):
    chosen = items[0]
    index = jnp.full(chosen.shape, index, jnp.int32)
    for i in range(1, len(items)):
        chosen = jnp.where(index == i, items[i], chosen)
    return chosen


def kernel(nr, nc, pivots_in, dist_in, ids_in, lens_in, out, pivots, dist, ids, lens, in_sem,
           e_all, ids_r, len_r, c_send, c_recv, c_all, c_full, r_recv, k_recv, t_ref, sems):
    rows_here, cols_here = dist.shape
    width = lens.shape[1]
    depth = e_all.shape[1]
    groups = cols_here // width
    half = rows_here // 2
    piece = half // nc
    pair = 2 * PIVOT
    devices = nr * nc
    r, c = lax.axis_index("row"), lax.axis_index("col")
    me = r * nc + c
    row_peers = [lax.rem(r + i, nr) for i in range(1, nr)]
    col_peers = [lax.rem(c + i, nc) for i in range(1, nc)]

    loads = [
        pltpu.make_async_copy(src, dst, in_sem.at[i])
        for i, (src, dst) in enumerate(
            [(pivots_in, pivots), (dist_in, dist), (lens_in, lens), (ids_in, ids)])
    ]
    for load in loads:
        load.start()

    barrier = pltpu.get_barrier_semaphore()

    def greet(i, carry):
        other = lax.rem(me + i, devices)
        pl.semaphore_signal(barrier, inc=1, device_id=(lax.div(other, nc), lax.rem(other, nc)),
                            device_id_type=MESH)
        return carry

    lax.fori_loop(1, devices, greet, 0)

    for load in loads:
        load.wait()
    p = [pivots[q] for q in range(2)]
    base = [p[q] * PIVOT for q in range(2)]
    row_root = [lax.div(base[q], rows_here) for q in range(2)]
    col_root = [lax.div(base[q], cols_here) for q in range(2)]
    row_slot = [lax.rem(p[q], rows_here // PIVOT) for q in range(2)]
    col_slot = [lax.rem(p[q], cols_here // PIVOT) for q in range(2)]
    row_cuts = [slice(i, i + PIVOT) for i in range(0, rows_here, PIVOT)]

    blocks = cols_here // PIVOT
    lane = lax.broadcasted_iota(jnp.int32, (1, cols_here), 1)
    source = jnp.where(
        lane // PIVOT % 2 == 0, jnp.full_like(lane, col_slot[0]), jnp.full_like(lane, col_slot[1]))
    turn = (lane // PIVOT - source + blocks) % blocks
    packed = jnp.zeros((half, cols_here), jnp.float32)
    for h in range(2):
        part = dist[h * half : (h + 1) * half, :]
        for g in range(blocks):
            turned = pltpu.roll(part, g * PIVOT, 1) if g else part
            packed = jnp.where((turn == g) & (lane // pair == h), turned, packed)
    for j in range(nc):
        c_send[j] = packed[j * piece : (j + 1) * piece, :]
    c_recv[c] = c_send[c]
    own_len = jnp.concatenate(
        [lens[...], jnp.zeros((groups * depth - NEIGHBORS, width), jnp.float32)], axis=0)
    e_all[me] = jnp.concatenate(
        [own_len[g * depth : (g + 1) * depth, :] for g in range(groups)], axis=1)
    for q in range(2):
        r_recv[r, q * PIVOT : (q + 1) * PIVOT, :] = pick([dist[cut, :] for cut in row_cuts], row_slot[q])

    pl.semaphore_wait(barrier, devices - 1)

    def send(src, dst, kind, peer):
        pltpu.make_async_remote_copy(
            src_ref=src, dst_ref=dst, send_sem=sems.at[kind, 0], recv_sem=sems.at[kind, 1],
            device_id=peer, device_id_type=MESH).start()

    def all_of(buffer, kind):
        count = buffer.shape[0] - 1
        every = buffer.at[pl.ds(0, count)]
        return pltpu.make_async_remote_copy(
            src_ref=every, dst_ref=every, send_sem=sems.at[kind, 0], recv_sem=sems.at[kind, 1],
            device_id=(lax.rem(r + 1, nr), c), device_id_type=MESH)

    for peer in col_peers:
        send(c_send.at[peer], c_recv.at[c], 0, (r, peer))

    def send_edges(i, carry):
        other = lax.rem(me + i, devices)
        send(e_all.at[me], e_all.at[me], 1, (lax.div(other, nc), lax.rem(other, nc)))
        return carry

    lax.fori_loop(1, devices, send_edges, 0)
    for peer in row_peers:
        send(r_recv.at[r], r_recv.at[r], 2, (peer, c))

    for t in range(0, rows_here, cols_here):
        start = pl.multiple_of(r * rows_here + t, cols_here)
        ids_r[t : t + cols_here, :] = ids[:, pl.ds(start, cols_here)].T
    ids_own = ids[:, pl.ds(pl.multiple_of(c * cols_here, cols_here), cols_here)]
    id_tiles = [ids[:, j * cols_here : (j + 1) * cols_here] for j in range(nc)]
    mixed = jnp.zeros_like(ids_own)
    for q in range(2):
        tile = pick(id_tiles, col_root[q])
        for g in range(blocks):
            turned = pltpu.roll(tile, g * PIVOT, 1) if g else tile
            mixed = jnp.where((turn == g) & (lane // PIVOT == q), turned, mixed)
    ids_p = mixed.T[0:pair, :]
    ids_cols = jnp.concatenate([ids_own, mixed], axis=1)
    at_s = lax.broadcasted_iota(jnp.int32, (pair, 1), 0)
    p_rows = jnp.where(at_s < PIVOT, base[0] + at_s, base[1] + at_s - PIVOT)
    p_cols = jnp.where(lane < PIVOT, base[0] + lane, base[1] + lane - PIVOT)
    col_ids = jnp.concatenate([c * cols_here + lane, p_cols], axis=1)

    all_of(c_recv, 0).wait_recv()
    arrived = [c_recv[j] for j in range(nc)]
    c_all[c] = jnp.where(lane % pair < PIVOT, pick(arrived, col_root[0]), pick(arrived, col_root[1]))
    for peer in col_peers:
        send(c_all.at[c], c_all.at[c], 3, (r, peer))

    all_of(e_all, 1).wait_recv()

    def spread(tiles):
        parts = []
        for g in range(-(-NEIGHBORS // depth)):
            part = jnp.zeros((depth, cols_here), jnp.float32)
            for i, tile in enumerate(tiles):
                turned = pltpu.roll(tile, (i - g) * width % cols_here, 1) if i != g else tile
                part = jnp.where(lane // width == i, turned, part)
            parts.append(part)
        return jnp.concatenate(parts, axis=0)

    for t in range(0, rows_here, cols_here):
        len_r[t : t + cols_here, :] = spread(
            [e_all[r * nc + t // width + i] for i in range(groups)])[0:NEIGHBORS].T
    len_own = spread([e_all[c * nr + i] for i in range(nr)])
    steps = PIVOT // width
    everyone = [e_all[i] for i in range(devices)]
    len_mixed = spread([pick(everyone, p[q] * steps + j) for q in range(2) for j in range(steps)])
    len_p = len_mixed[0:NEIGHBORS].T[0:pair, :]
    len_cols = jnp.concatenate([len_own, len_mixed], axis=1)

    p_bound = edge_bound(p_rows, col_ids, ids_p, len_p, ids_cols, len_cols)
    all_of(r_recv, 2).wait_recv()
    rows_panel = jnp.concatenate(
        [pick([r_recv[i, q * PIVOT : (q + 1) * PIVOT, :] for i in range(nr)], row_root[q])
         for q in range(2)], axis=0)
    rows_panel = jnp.minimum(rows_panel, p_bound[:, 0:cols_here])

    all_of(c_all, 3).wait_recv()
    cols_packed = jnp.concatenate([c_all[j] for j in range(nc)], axis=0)
    c_full[0:half, :] = cols_packed
    c_full[half:rows_here, :] = pltpu.roll(cols_packed, pair, 1)
    cuts = [c_full[cut, :] for cut in row_cuts]
    second = pltpu.roll(pick(cuts, row_slot[1]), pair, 1)
    k_recv[r] = jnp.where(lane < pair, pick(cuts, row_slot[0]), second)
    for peer in row_peers:
        send(k_recv.at[r], k_recv.at[r], 4, (peer, c))

    def start_rows(b, carry):
        at = pl.ds(pl.multiple_of(b * PIVOT, PIVOT), PIVOT)
        row_ids = r * rows_here + b * PIVOT + lax.broadcasted_iota(jnp.int32, (PIVOT, 1), 0)
        bound = edge_bound(row_ids, col_ids, ids_r[at, :], len_r[at, :], ids_cols, len_cols)
        out[at, :] = jnp.minimum(dist[at, :], bound[:, 0:cols_here])
        c_full[at, :] = jnp.minimum(c_full[at, :], bound[:, cols_here:])
        return carry

    lax.fori_loop(0, rows_here // PIVOT, start_rows, 0)

    all_of(k_recv, 4).wait_recv()
    corner = jnp.concatenate(
        [pick([k_recv[i] for i in range(nr)], row_root[q])[:, q * pair : (q + 1) * pair]
         for q in range(2)], axis=0)
    corner = jnp.minimum(corner, p_bound[:, cols_here : cols_here + pair])
    corner = lax.fori_loop(0, 6, lambda _, a: minplus(None, a, a), corner)
    t_ref[...] = minplus(None, corner, rows_panel)

    def finish(b, carry):
        at = pl.ds(pl.multiple_of(b * PIVOT, PIVOT), PIVOT)
        out[at, :] = minplus(out[at, :], c_full[at, 0:pair], t_ref[...])
        return carry

    lax.fori_loop(0, rows_here // PIVOT, finish, 0)
    for kind, buffer in enumerate([c_recv, e_all, r_recv, c_all, k_recv]):
        all_of(buffer, kind).wait_send()


def on_device(nr, nc, distances, neighbor_ids, edge_lengths, pivots):
    rows_here, cols_here = distances.shape
    half = rows_here // 2
    piece = half // nc
    depth = pl.next_power_of_2(pl.cdiv(NEIGHBORS, cols_here // edge_lengths.shape[1]))
    vmem = pl.BlockSpec(memory_space=pltpu.VMEM)
    f32 = jnp.float32
    dma = pltpu.SemaphoreType.DMA
    return pl.pallas_call(
        functools.partial(kernel, nr, nc),
        out_shape=jax.ShapeDtypeStruct(distances.shape, f32),
        in_specs=[pl.BlockSpec(memory_space=pltpu.HBM)] * 4,
        out_specs=vmem,
        scratch_shapes=[
            pltpu.SMEM(pivots.shape, jnp.int32),
            pltpu.VMEM(distances.shape, f32),
            pltpu.VMEM(neighbor_ids.shape, jnp.int32),
            pltpu.VMEM(edge_lengths.shape, f32),
            dma((4,)),
            pltpu.VMEM((nr * nc, depth, cols_here), f32),
            pltpu.VMEM((rows_here, NEIGHBORS), jnp.int32),
            pltpu.VMEM((rows_here, NEIGHBORS), f32),
            pltpu.VMEM((nc, piece, cols_here), f32),
            pltpu.VMEM((nc, piece, cols_here), f32),
            pltpu.VMEM((nc, piece, cols_here), f32),
            pltpu.VMEM((rows_here, cols_here), f32),
            pltpu.VMEM((nr, 2 * PIVOT, cols_here), f32),
            pltpu.VMEM((nr, PIVOT, cols_here), f32),
            pltpu.VMEM((2 * PIVOT, cols_here), f32),
            dma((5, 2)),
        ],
        compiler_params=pltpu.CompilerParams(
            collective_id=0, has_side_effects=True, vmem_limit_bytes=60 * 1024 * 1024),
    )(pivots, distances, neighbor_ids, edge_lengths)


def solution(mesh):
    placed = (P("row", "col"), P(), P(None, ("row", "col")), P())
    body = functools.partial(on_device, mesh.shape["row"], mesh.shape["col"])
    return jax.shard_map(
        body, mesh=mesh, in_specs=placed, out_specs=P("row", "col"), check_vma=False
    )
```

time: 28.6 us -> 28.6 us (level)
  no operation moved by 1% of the time
where the time goes in v4:
time: 28.6 us; the launch traced here: 28.4 us
  Pallas kernels  26.8 us (94%)
  local copies, waits for them, and re-layouts  1.57 us (5%)
    pallas_call x1, Pallas kernels, on_device(): pl.pallas_call(functools.partial(kernel, nr, nc), out_shape=jax.ShapeDtyp...  26.8 us
    unnamed x1, local copies, waits for them, and re-layouts  1.57 us

profile of v4, /device:TPU:0, one launch (start us, length us, event | category | flops | bytes accessed | tf_op | source)
XLA Modules:
  0.0 28.4 jit_solution(18115873069292174843)
XLA Ops:
  0.0 26.8 %shard_map.46 = f32[256,128]{1,0:T(8,128)} custom-call(s32[2]{0:T(128)} %pivots_in.1, f32[256,128]{1,0:T(8,128)} %dist_in.1, s32[10,1024]{1,0:T(8,128)} %ids_in.1, f32[10,32]{1,0:T(8,128)} %lens_in.1), custom_call_target="tpu_custom_call" | custom-call | tf_op jit(solution)/shard_map/pallas_call | solution.py:228
  26.8 1.6 %copy.6 = f32[256,128]{1,0:T(8,128)} copy(f32[256,128]{1,0:T(8,128)} %shard_map.46) | data formatting | bytes 262144

commit v5 on v4

--- a/solution.py
+++ b/solution.py
@@ -37,7 +37,7 @@
 
 
 def kernel(nr, nc, pivots_in, dist_in, ids_in, lens_in, out, pivots, dist, ids, lens, in_sem,
-           e_all, ids_r, len_r, c_send, c_recv, c_all, c_full, r_recv, k_recv, t_ref, sems):
+           e_send, e_all, ids_r, len_r, c_send, c_recv, c_all, c_full, r_recv, k_all, k_ref, t_ref, sems):
     rows_here, cols_here = dist.shape
     width = lens.shape[1]
     depth = e_all.shape[1]
@@ -95,10 +95,23 @@
     c_recv[c] = c_send[c]
     own_len = jnp.concatenate(
         [lens[...], jnp.zeros((groups * depth - NEIGHBORS, width), jnp.float32)], axis=0)
-    e_all[me] = jnp.concatenate(
+    own_len = jnp.concatenate(
         [own_len[g * depth : (g + 1) * depth, :] for g in range(groups)], axis=1)
-    for q in range(2):
-        r_recv[r, q * PIVOT : (q + 1) * PIVOT, :] = pick([dist[cut, :] for cut in row_cuts], row_slot[q])
+    own_rows = jnp.concatenate(
+        [pick([dist[cut, :] for cut in row_cuts], row_slot[q]) for q in range(2)], axis=0)
+    r_recv[r] = own_rows
+    own_corner = own_rows
+    for g in range(1, blocks):
+        turned = pltpu.roll(own_rows, g * PIVOT, 1)
+        own_corner = jnp.where((turn == g) & (lane < pair), turned, own_corner)
+    last = groups - 1
+    levels = pair // depth
+    for part in range(pair // width):
+        turned = pltpu.roll(own_corner, (last - part) * width % cols_here, 1)
+        for m in range(levels):
+            e_send[part * levels + m] = jnp.where(
+                lane // width == last, turned[m * depth : (m + 1) * depth, :], own_len)
+    e_all[me] = e_send[me]
 
     pl.semaphore_wait(barrier, devices - 1)
 
@@ -114,15 +127,14 @@
             src_ref=every, dst_ref=every, send_sem=sems.at[kind, 0], recv_sem=sems.at[kind, 1],
             device_id=(lax.rem(r + 1, nr), c), device_id_type=MESH)
 
+    def send_edges(i, carry):
+        other = lax.rem(me + i, devices)
+        send(e_send.at[other], e_all.at[me], 1, (lax.div(other, nc), lax.rem(other, nc)))
+        return carry
+
+    lax.fori_loop(1, devices, send_edges, 0)
     for peer in col_peers:
         send(c_send.at[peer], c_recv.at[c], 0, (r, peer))
-
-    def send_edges(i, carry):
-        other = lax.rem(me + i, devices)
-        send(e_all.at[me], e_all.at[me], 1, (lax.div(other, nc), lax.rem(other, nc)))
-        return carry
-
-    lax.fori_loop(1, devices, send_edges, 0)
     for peer in row_peers:
         send(r_recv.at[r], r_recv.at[r], 2, (peer, c))
 
@@ -144,13 +156,32 @@
     p_cols = jnp.where(lane < PIVOT, base[0] + lane, base[1] + lane - PIVOT)
     col_ids = jnp.concatenate([c * cols_here + lane, p_cols], axis=1)
 
+    all_of(e_all, 1).wait_recv()
+    everyone = [e_all[i] for i in range(devices)]
+    in_first_row = lax.rem(me, levels) * depth < PIVOT
+    in_first_col = lax.div(me, levels) * width < PIVOT
+    owner = (jnp.where(in_first_row, row_root[0], row_root[1]) * nc
+             + jnp.where(in_first_col, col_root[0], col_root[1]))
+    mine = pick(everyone, owner)
+    flat = jnp.zeros((1, cols_here), jnp.float32)
+    for i in range(depth):
+        turned = mine[i : i + 1, :]
+        if i != last:
+            turned = pltpu.roll(turned, (i - last) * width % cols_here, 1)
+        flat = jnp.where(lane // width == i, turned, flat)
+    k_all[me] = flat
+
+    def send_corner(i, carry):
+        other = lax.rem(me + i, devices)
+        send(k_all.at[me], k_all.at[me], 4, (lax.div(other, nc), lax.rem(other, nc)))
+        return carry
+
+    lax.fori_loop(1, devices, send_corner, 0)
     all_of(c_recv, 0).wait_recv()
     arrived = [c_recv[j] for j in range(nc)]
     c_all[c] = jnp.where(lane % pair < PIVOT, pick(arrived, col_root[0]), pick(arrived, col_root[1]))
     for peer in col_peers:
         send(c_all.at[c], c_all.at[c], 3, (r, peer))
-
-    all_of(e_all, 1).wait_recv()
 
     def spread(tiles):
         parts = []
@@ -167,7 +198,6 @@
             [e_all[r * nc + t // width + i] for i in range(groups)])[0:NEIGHBORS].T
     len_own = spread([e_all[c * nr + i] for i in range(nr)])
     steps = PIVOT // width
-    everyone = [e_all[i] for i in range(devices)]
     len_mixed = spread([pick(everyone, p[q] * steps + j) for q in range(2) for j in range(steps)])
     len_p = len_mixed[0:NEIGHBORS].T[0:pair, :]
     len_cols = jnp.concatenate([len_own, len_mixed], axis=1)
@@ -179,41 +209,44 @@
          for q in range(2)], axis=0)
     rows_panel = jnp.minimum(rows_panel, p_bound[:, 0:cols_here])
 
-    all_of(c_all, 3).wait_recv()
-    cols_packed = jnp.concatenate([c_all[j] for j in range(nc)], axis=0)
-    c_full[0:half, :] = cols_packed
-    c_full[half:rows_here, :] = pltpu.roll(cols_packed, pair, 1)
-    cuts = [c_full[cut, :] for cut in row_cuts]
-    second = pltpu.roll(pick(cuts, row_slot[1]), pair, 1)
-    k_recv[r] = jnp.where(lane < pair, pick(cuts, row_slot[0]), second)
-    for peer in row_peers:
-        send(k_recv.at[r], k_recv.at[r], 4, (peer, c))
-
     def start_rows(b, carry):
         at = pl.ds(pl.multiple_of(b * PIVOT, PIVOT), PIVOT)
         row_ids = r * rows_here + b * PIVOT + lax.broadcasted_iota(jnp.int32, (PIVOT, 1), 0)
         bound = edge_bound(row_ids, col_ids, ids_r[at, :], len_r[at, :], ids_cols, len_cols)
         out[at, :] = jnp.minimum(dist[at, :], bound[:, 0:cols_here])
-        c_full[at, :] = jnp.minimum(c_full[at, :], bound[:, cols_here:])
+        c_full[at, :] = bound[:, cols_here:]
         return carry
 
     lax.fori_loop(0, rows_here // PIVOT, start_rows, 0)
 
-    all_of(k_recv, 4).wait_recv()
-    corner = jnp.concatenate(
-        [pick([k_recv[i] for i in range(nr)], row_root[q])[:, q * pair : (q + 1) * pair]
-         for q in range(2)], axis=0)
+    all_of(k_all, 4).wait_recv()
+    gathered = jnp.concatenate([k_all[i] for i in range(devices)], axis=0)
+    for i in range(depth):
+        rows = jnp.zeros((levels, cols_here), jnp.float32)
+        for part in range(pair // width):
+            turned = gathered[part * levels : (part + 1) * levels, :]
+            if part != i:
+                turned = pltpu.roll(turned, (part - i) * width % cols_here, 1)
+            rows = jnp.where(lane // width == part, turned, rows)
+        k_ref[pl.ds(i, levels, stride=depth), :] = rows
+    corner = k_ref[:, 0:pair]
     corner = jnp.minimum(corner, p_bound[:, cols_here : cols_here + pair])
     corner = lax.fori_loop(0, 6, lambda _, a: minplus(None, a, a), corner)
     t_ref[...] = minplus(None, corner, rows_panel)
 
+    all_of(c_all, 3).wait_recv()
+    cols_packed = jnp.concatenate([c_all[j] for j in range(nc)], axis=0)
+    c_full[0:half, :] = jnp.minimum(c_full[0:half, :], cols_packed)
+    c_full[half:rows_here, :] = jnp.minimum(
+        c_full[half:rows_here, :], pltpu.roll(cols_packed, pair, 1))
+
     def finish(b, carry):
         at = pl.ds(pl.multiple_of(b * PIVOT, PIVOT), PIVOT)
         out[at, :] = minplus(out[at, :], c_full[at, 0:pair], t_ref[...])
         return carry
 
     lax.fori_loop(0, rows_here // PIVOT, finish, 0)
-    for kind, buffer in enumerate([c_recv, e_all, r_recv, c_all, k_recv]):
+    for kind, buffer in enumerate([c_recv, e_all, r_recv, c_all, k_all]):
         all_of(buffer, kind).wait_send()
 
 
@@ -237,6 +270,7 @@
             pltpu.VMEM(edge_lengths.shape, f32),
             dma((4,)),
             pltpu.VMEM((nr * nc, depth, cols_here), f32),
+            pltpu.VMEM((nr * nc, depth, cols_here), f32),
             pltpu.VMEM((rows_here, NEIGHBORS), jnp.int32),
             pltpu.VMEM((rows_here, NEIGHBORS), f32),
             pltpu.VMEM((nc, piece, cols_here), f32),
@@ -244,7 +278,8 @@
             pltpu.VMEM((nc, piece, cols_here), f32),
             pltpu.VMEM((rows_here, cols_here), f32),
             pltpu.VMEM((nr, 2 * PIVOT, cols_here), f32),
-            pltpu.VMEM((nr, PIVOT, cols_here), f32),
+            pltpu.VMEM((nr * nc, 1, cols_here), f32),
+            pltpu.VMEM((2 * PIVOT, cols_here), f32),
             pltpu.VMEM((2 * PIVOT, cols_here), f32),
             dma((5, 2)),
         ],

time: 28.6 us -> 27.8 us (0.972)
  Pallas kernels: 26.8 us -> 26.1 us
    pallas_call x1, Pallas kernels: 26.8 us -> 26.1 us  [on_device(): pl.pallas_call(functools.partial(kernel, nr, nc), out_shape=jax.ShapeDtyp...]
where the time goes in v5:
time: 27.8 us; the launch traced here: 27.7 us
  Pallas kernels  26.1 us (94%)
  local copies, waits for them, and re-layouts  1.57 us (6%)
    pallas_call x1, Pallas kernels, on_device(): pl.pallas_call(functools.partial(kernel, nr, nc), out_shape=jax.ShapeDtyp...  26.1 us
    unnamed x1, local copies, waits for them, and re-layouts  1.57 us

profile of v5, /device:TPU:0, one launch (start us, length us, event | category | flops | bytes accessed | tf_op | source)
XLA Modules:
  0.0 27.7 jit_solution(12862699365981201054)
XLA Ops:
  0.0 26.1 %shard_map.46 = f32[256,128]{1,0:T(8,128)} custom-call(s32[2]{0:T(128)} %pivots_in.1, f32[256,128]{1,0:T(8,128)} %dist_in.1, s32[10,1024]{1,0:T(8,128)} %ids_in.1, f32[10,32]{1,0:T(8,128)} %lens_in.1), custom_call_target="tpu_custom_call" | custom-call | tf_op jit(solution)/shard_map/pallas_call | solution.py:261
  26.1 1.6 %copy.6 = f32[256,128]{1,0:T(8,128)} copy(f32[256,128]{1,0:T(8,128)} %shard_map.46) | data formatting | bytes 262144

commit v6 on v5

--- a/solution.py
+++ b/solution.py
@@ -26,6 +26,18 @@
         term = left[:, k : k + 1] + right[k : k + 1, :]
         total = term if total is None else jnp.minimum(total, term)
     return total
+
+
+def square(twice):
+    size = twice.shape[0]
+    lane = lax.broadcasted_iota(jnp.int32, twice.shape, 1)
+    rows = jnp.where(lane[: size // 2] < size, twice[: size // 2], twice[size // 2 :])
+    total = twice
+    for k in range(size // 2):
+        inner = jnp.where(lane < size, k, k + size // 2)
+        left = jnp.take_along_axis(twice, inner, axis=1, mode="promise_in_bounds")
+        total = jnp.minimum(total, left + rows[k : k + 1, :])
+    return jnp.minimum(total, pltpu.roll(total, size, 1))
 
 
 def pick(items, index):
@@ -231,7 +243,8 @@
         k_ref[pl.ds(i, levels, stride=depth), :] = rows
     corner = k_ref[:, 0:pair]
     corner = jnp.minimum(corner, p_bound[:, cols_here : cols_here + pair])
-    corner = lax.fori_loop(0, 6, lambda _, a: minplus(None, a, a), corner)
+    corner = jnp.concatenate([corner, corner], axis=1)
+    corner = lax.fori_loop(0, 6, lambda _, a: square(a), corner)[:, 0:pair]
     t_ref[...] = minplus(None, corner, rows_panel)
 
     all_of(c_all, 3).wait_recv()

time: 27.8 us -> 26.7 us (0.960)
  Pallas kernels: 26.1 us -> 25 us
    pallas_call x1, Pallas kernels: 26.1 us -> 25 us  [on_device(): pl.pallas_call(functools.partial(kernel, nr, nc), out_shape=jax.ShapeDtyp...]
where the time goes in v6:
time: 26.7 us; the launch traced here: 26.5 us
  Pallas kernels  25 us (94%)
  local copies, waits for them, and re-layouts  1.57 us (6%)
    pallas_call x1, Pallas kernels, on_device(): pl.pallas_call(functools.partial(kernel, nr, nc), out_shape=jax.ShapeDtyp...  25 us
    unnamed x1, local copies, waits for them, and re-layouts  1.57 us

profile of v6, /device:TPU:0, one launch (start us, length us, event | category | flops | bytes accessed | tf_op | source)
XLA Modules:
  0.0 26.5 jit_solution(13601169523239434774)
XLA Ops:
  0.0 25.0 %shard_map.46 = f32[256,128]{1,0:T(8,128)} custom-call(s32[2]{0:T(128)} %pivots_in.1, f32[256,128]{1,0:T(8,128)} %dist_in.1, s32[10,1024]{1,0:T(8,128)} %ids_in.1, f32[10,32]{1,0:T(8,128)} %lens_in.1), custom_call_target="tpu_custom_call" | custom-call | tf_op jit(solution)/shard_map/pallas_call | solution.py:274
  25.0 1.6 %copy.6 = f32[256,128]{1,0:T(8,128)} copy(f32[256,128]{1,0:T(8,128)} %shard_map.46) | data formatting | bytes 262144

commit v7 on v6

--- a/solution.py
+++ b/solution.py
@@ -73,13 +73,23 @@
 
     barrier = pltpu.get_barrier_semaphore()
 
-    def greet(i, carry):
-        other = lax.rem(me + i, devices)
-        pl.semaphore_signal(barrier, inc=1, device_id=(lax.div(other, nc), lax.rem(other, nc)),
-                            device_id_type=MESH)
-        return carry
-
-    lax.fori_loop(1, devices, greet, 0)
+    def every_peer(act):
+        if devices > 64:
+
+            def step(i, carry):
+                other = lax.rem(me + i, devices)
+                act(lax.div(other, nc), lax.rem(other, nc))
+                return carry
+
+            lax.fori_loop(1, devices, step, 0)
+            return
+        for i in range(nr):
+            for j in range(nc):
+                if i or j:
+                    act(row_peers[i - 1] if i else r, col_peers[j - 1] if j else c)
+
+    every_peer(lambda row, col: pl.semaphore_signal(
+        barrier, inc=1, device_id=(row, col), device_id_type=MESH))
 
     for load in loads:
         load.wait()
@@ -139,12 +149,7 @@
             src_ref=every, dst_ref=every, send_sem=sems.at[kind, 0], recv_sem=sems.at[kind, 1],
             device_id=(lax.rem(r + 1, nr), c), device_id_type=MESH)
 
-    def send_edges(i, carry):
-        other = lax.rem(me + i, devices)
-        send(e_send.at[other], e_all.at[me], 1, (lax.div(other, nc), lax.rem(other, nc)))
-        return carry
-
-    lax.fori_loop(1, devices, send_edges, 0)
+    every_peer(lambda row, col: send(e_send.at[row * nc + col], e_all.at[me], 1, (row, col)))
     for peer in col_peers:
         send(c_send.at[peer], c_recv.at[c], 0, (r, peer))
     for peer in row_peers:
@@ -183,12 +188,7 @@
         flat = jnp.where(lane // width == i, turned, flat)
     k_all[me] = flat
 
-    def send_corner(i, carry):
-        other = lax.rem(me + i, devices)
-        send(k_all.at[me], k_all.at[me], 4, (lax.div(other, nc), lax.rem(other, nc)))
-        return carry
-
-    lax.fori_loop(1, devices, send_corner, 0)
+    every_peer(lambda row, col: send(k_all.at[me], k_all.at[me], 4, (row, col)))
     all_of(c_recv, 0).wait_recv()
     arrived = [c_recv[j] for j in range(nc)]
     c_all[c] = jnp.where(lane % pair < PIVOT, pick(arrived, col_root[0]), pick(arrived, col_root[1]))
@@ -297,8 +297,9 @@
             dma((5, 2)),
         ],
         compiler_params=pltpu.CompilerParams(
-            collective_id=0, has_side_effects=True, vmem_limit_bytes=60 * 1024 * 1024),
-    )(pivots, distances, neighbor_ids, edge_lengths)
+            collective_id=0, has_side_effects=True, vmem_limit_bytes=32 * 1024 * 1024),
+    )(*[pltpu.with_memory_space_constraint(x, pltpu.HBM)
+        for x in (pivots, distances, neighbor_ids, edge_lengths)])
 
 
 def solution(mesh):

time: 26.7 us -> 25.2 us (0.944)
  local copies, waits for them, and re-layouts: 1.57 us -> 0.66 us
  Pallas kernels: 25 us -> 24.4 us
    unnamed x1, local copies, waits for them, and re-layouts: 1.57 us -> 0.66 us
    pallas_call x1, Pallas kernels: 25 us -> 24.4 us  [on_device(): pl.pallas_call(functools.partial(kernel, nr, nc), out_shape=jax.ShapeDtyp...]
where the time goes in v7:
time: 25.2 us; the launch traced here: 25 us
  Pallas kernels  24.4 us (97%)
  local copies, waits for them, and re-layouts  0.66 us (3%)
    pallas_call x1, Pallas kernels, on_device(): pl.pallas_call(functools.partial(kernel, nr, nc), out_shape=jax.ShapeDtyp...  24.4 us
    unnamed x1, local copies, waits for them, and re-layouts  0.66 us

profile of v7, /device:TPU:0, one launch (start us, length us, event | category | flops | bytes accessed | tf_op | source)
XLA Modules:
  0.0 25.0 jit_solution(18002370907432828874)
XLA Ops:
  0.0 24.4 %shard_map.46 = f32[256,128]{1,0:T(8,128)S(1)} custom-call(s32[2]{0:T(128)} %pivots_in.1, f32[256,128]{1,0:T(8,128)} %dist_in.1, s32[10,1024]{1,0:T(8,128)} %ids_in.1, f32[10,32]{1,0:T(8,128)} %lens_in.1), custom_call_target="tpu_custom_call" | custom-call | tf_op jit(solution)/shard_map/pallas_call | solution.py:274
  24.4 0.7 %copy.6 = f32[256,128]{1,0:T(8,128)} copy(f32[256,128]{1,0:T(8,128)S(1)} %shard_map.46) | data formatting | bytes 262144

commit v8 on v7

--- a/solution.py
+++ b/solution.py
@@ -28,15 +28,15 @@
     return total
 
 
-def square(twice):
+def square(twice, rows_ref):
     size = twice.shape[0]
     lane = lax.broadcasted_iota(jnp.int32, twice.shape, 1)
-    rows = jnp.where(lane[: size // 2] < size, twice[: size // 2], twice[size // 2 :])
+    rows_ref[...] = jnp.where(lane[: size // 2] < size, twice[: size // 2], twice[size // 2 :])
     total = twice
     for k in range(size // 2):
         inner = jnp.where(lane < size, k, k + size // 2)
         left = jnp.take_along_axis(twice, inner, axis=1, mode="promise_in_bounds")
-        total = jnp.minimum(total, left + rows[k : k + 1, :])
+        total = jnp.minimum(total, left + rows_ref[k : k + 1, :])
     return jnp.minimum(total, pltpu.roll(total, size, 1))
 
 
@@ -106,15 +106,6 @@
     source = jnp.where(
         lane // PIVOT % 2 == 0, jnp.full_like(lane, col_slot[0]), jnp.full_like(lane, col_slot[1]))
     turn = (lane // PIVOT - source + blocks) % blocks
-    packed = jnp.zeros((half, cols_here), jnp.float32)
-    for h in range(2):
-        part = dist[h * half : (h + 1) * half, :]
-        for g in range(blocks):
-            turned = pltpu.roll(part, g * PIVOT, 1) if g else part
-            packed = jnp.where((turn == g) & (lane // pair == h), turned, packed)
-    for j in range(nc):
-        c_send[j] = packed[j * piece : (j + 1) * piece, :]
-    c_recv[c] = c_send[c]
     own_len = jnp.concatenate(
         [lens[...], jnp.zeros((groups * depth - NEIGHBORS, width), jnp.float32)], axis=0)
     own_len = jnp.concatenate(
@@ -150,6 +141,15 @@
             device_id=(lax.rem(r + 1, nr), c), device_id_type=MESH)
 
     every_peer(lambda row, col: send(e_send.at[row * nc + col], e_all.at[me], 1, (row, col)))
+    packed = jnp.zeros((half, cols_here), jnp.float32)
+    for h in range(2):
+        part = dist[h * half : (h + 1) * half, :]
+        for g in range(blocks):
+            turned = pltpu.roll(part, g * PIVOT, 1) if g else part
+            packed = jnp.where((turn == g) & (lane // pair == h), turned, packed)
+    for j in range(nc):
+        c_send[j] = packed[j * piece : (j + 1) * piece, :]
+    c_recv[c] = c_send[c]
     for peer in col_peers:
         send(c_send.at[peer], c_recv.at[c], 0, (r, peer))
     for peer in row_peers:
@@ -244,8 +244,9 @@
     corner = k_ref[:, 0:pair]
     corner = jnp.minimum(corner, p_bound[:, cols_here : cols_here + pair])
     corner = jnp.concatenate([corner, corner], axis=1)
-    corner = lax.fori_loop(0, 6, lambda _, a: square(a), corner)[:, 0:pair]
-    t_ref[...] = minplus(None, corner, rows_panel)
+    corner = lax.fori_loop(0, 6, lambda _, a: square(a, t_ref.at[0:PIVOT, :]), corner)[:, 0:pair]
+    k_ref[...] = rows_panel
+    t_ref[...] = minplus(None, corner, k_ref)
 
     all_of(c_all, 3).wait_recv()
     cols_packed = jnp.concatenate([c_all[j] for j in range(nc)], axis=0)
@@ -255,7 +256,7 @@
 
     def finish(b, carry):
         at = pl.ds(pl.multiple_of(b * PIVOT, PIVOT), PIVOT)
-        out[at, :] = minplus(out[at, :], c_full[at, 0:pair], t_ref[...])
+        out[at, :] = minplus(out[at, :], c_full[at, 0:pair], t_ref)
         return carry
 
     lax.fori_loop(0, rows_here // PIVOT, finish, 0)

time: 25.2 us -> 25.2 us (level)
  no operation moved by 1% of the time
where the time goes in v8:
time: 25.2 us; the launch traced here: 25 us
  Pallas kernels  24.4 us (97%)
  local copies, waits for them, and re-layouts  0.66 us (3%)
    pallas_call x1, Pallas kernels, on_device(): pl.pallas_call(functools.partial(kernel, nr, nc), out_shape=jax.ShapeDtyp...  24.4 us
    unnamed x1, local copies, waits for them, and re-layouts  0.66 us

profile of v8, /device:TPU:0, one launch (start us, length us, event | category | flops | bytes accessed | tf_op | source)
XLA Modules:
  0.0 25.0 jit_solution(13971264048498461108)
XLA Ops:
  0.0 24.4 %shard_map.46 = f32[256,128]{1,0:T(8,128)S(1)} custom-call(s32[2]{0:T(128)} %pivots_in.1, f32[256,128]{1,0:T(8,128)} %dist_in.1, s32[10,1024]{1,0:T(8,128)} %ids_in.1, f32[10,32]{1,0:T(8,128)} %lens_in.1), custom_call_target="tpu_custom_call" | custom-call | tf_op jit(solution)/shard_map/pallas_call | solution.py:275
  24.4 0.7 %copy.6 = f32[256,128]{1,0:T(8,128)} copy(f32[256,128]{1,0:T(8,128)S(1)} %shard_map.46) | data formatting | bytes 262144

commit v9 on v8

--- a/solution.py
+++ b/solution.py
@@ -19,13 +19,6 @@
         backward = jnp.where(row_ids == ids_cols[k : k + 1, :], len_cols[k : k + 1, :], jnp.inf)
         bound = jnp.minimum(bound, jnp.minimum(forward, backward))
     return bound
-
-
-def minplus(total, left, right):
-    for k in range(left.shape[1]):
-        term = left[:, k : k + 1] + right[k : k + 1, :]
-        total = term if total is None else jnp.minimum(total, term)
-    return total
 
 
 def square(twice, rows_ref):
@@ -49,7 +42,7 @@
 
 
 def kernel(nr, nc, pivots_in, dist_in, ids_in, lens_in, out, pivots, dist, ids, lens, in_sem,
-           e_send, e_all, ids_r, len_r, c_send, c_recv, c_all, c_full, r_recv, k_all, k_ref, t_ref, sems):
+           e_send, e_all, ids_r, len_r, c_send, c_recv, c_all, left, r_recv, k_all, k_ref, work, id_ref, bounds, sems):
     rows_here, cols_here = dist.shape
     width = lens.shape[1]
     depth = e_all.shape[1]
@@ -74,7 +67,7 @@
     barrier = pltpu.get_barrier_semaphore()
 
     def every_peer(act):
-        if devices > 64:
+        if devices > 1:
 
             def step(i, carry):
                 other = lax.rem(me + i, devices)
@@ -157,7 +150,7 @@
 
     for t in range(0, rows_here, cols_here):
         start = pl.multiple_of(r * rows_here + t, cols_here)
-        ids_r[t : t + cols_here, :] = ids[:, pl.ds(start, cols_here)].T
+        ids_r[pair + t : pair + t + cols_here, :] = ids[:, pl.ds(start, cols_here)].T
     ids_own = ids[:, pl.ds(pl.multiple_of(c * cols_here, cols_here), cols_here)]
     id_tiles = [ids[:, j * cols_here : (j + 1) * cols_here] for j in range(nc)]
     mixed = jnp.zeros_like(ids_own)
@@ -166,10 +159,11 @@
         for g in range(blocks):
             turned = pltpu.roll(tile, g * PIVOT, 1) if g else tile
             mixed = jnp.where((turn == g) & (lane // PIVOT == q), turned, mixed)
-    ids_p = mixed.T[0:pair, :]
+    ids_r[0:pair, :] = mixed.T[0:pair, :]
     ids_cols = jnp.concatenate([ids_own, mixed], axis=1)
     at_s = lax.broadcasted_iota(jnp.int32, (pair, 1), 0)
-    p_rows = jnp.where(at_s < PIVOT, base[0] + at_s, base[1] + at_s - PIVOT)
+    id_ref[0:pair, :] = jnp.where(at_s < PIVOT, base[0] + at_s, base[1] + at_s - PIVOT)
+    id_ref[pair:, :] = r * rows_here + lax.broadcasted_iota(jnp.int32, (rows_here, 1), 0)
     p_cols = jnp.where(lane < PIVOT, base[0] + lane, base[1] + lane - PIVOT)
     col_ids = jnp.concatenate([c * cols_here + lane, p_cols], axis=1)
 
@@ -206,30 +200,30 @@
         return jnp.concatenate(parts, axis=0)
 
     for t in range(0, rows_here, cols_here):
-        len_r[t : t + cols_here, :] = spread(
+        len_r[pair + t : pair + t + cols_here, :] = spread(
             [e_all[r * nc + t // width + i] for i in range(groups)])[0:NEIGHBORS].T
     len_own = spread([e_all[c * nr + i] for i in range(nr)])
     steps = PIVOT // width
     len_mixed = spread([pick(everyone, p[q] * steps + j) for q in range(2) for j in range(steps)])
-    len_p = len_mixed[0:NEIGHBORS].T[0:pair, :]
+    len_r[0:pair, :] = len_mixed[0:NEIGHBORS].T[0:pair, :]
     len_cols = jnp.concatenate([len_own, len_mixed], axis=1)
 
-    p_bound = edge_bound(p_rows, col_ids, ids_p, len_p, ids_cols, len_cols)
+    def bound_rows(b, carry):
+        at = pl.ds(pl.multiple_of(b * PIVOT, PIVOT), PIVOT)
+        bounds[at, :] = edge_bound(
+            id_ref[at, :], col_ids, ids_r[at, :], len_r[at, :], ids_cols, len_cols)
+        return carry
+
+    lax.fori_loop(0, (pair + rows_here) // PIVOT, bound_rows, 0)
+
     all_of(r_recv, 2).wait_recv()
     rows_panel = jnp.concatenate(
         [pick([r_recv[i, q * PIVOT : (q + 1) * PIVOT, :] for i in range(nr)], row_root[q])
          for q in range(2)], axis=0)
-    rows_panel = jnp.minimum(rows_panel, p_bound[:, 0:cols_here])
-
-    def start_rows(b, carry):
-        at = pl.ds(pl.multiple_of(b * PIVOT, PIVOT), PIVOT)
-        row_ids = r * rows_here + b * PIVOT + lax.broadcasted_iota(jnp.int32, (PIVOT, 1), 0)
-        bound = edge_bound(row_ids, col_ids, ids_r[at, :], len_r[at, :], ids_cols, len_cols)
-        out[at, :] = jnp.minimum(dist[at, :], bound[:, 0:cols_here])
-        c_full[at, :] = bound[:, cols_here:]
-        return carry
-
-    lax.fori_loop(0, rows_here // PIVOT, start_rows, 0)
+    rows_panel = jnp.minimum(rows_panel, bounds[0:pair, 0:cols_here])
+    work[0:pair, :] = rows_panel
+    work[pair : 2 * pair, :] = rows_panel
+    work[2 * pair :, :] = jnp.minimum(dist[...], bounds[pair:, 0:cols_here])
 
     all_of(k_all, 4).wait_recv()
     gathered = jnp.concatenate([k_all[i] for i in range(devices)], axis=0)
@@ -242,24 +236,30 @@
             rows = jnp.where(lane // width == part, turned, rows)
         k_ref[pl.ds(i, levels, stride=depth), :] = rows
     corner = k_ref[:, 0:pair]
-    corner = jnp.minimum(corner, p_bound[:, cols_here : cols_here + pair])
+    corner = jnp.minimum(corner, bounds[0:pair, cols_here : cols_here + pair])
     corner = jnp.concatenate([corner, corner], axis=1)
-    corner = lax.fori_loop(0, 6, lambda _, a: square(a, t_ref.at[0:PIVOT, :]), corner)[:, 0:pair]
-    k_ref[...] = rows_panel
-    t_ref[...] = minplus(None, corner, k_ref)
+    corner = lax.fori_loop(0, 6, lambda _, a: square(a, k_ref.at[0:PIVOT, :]), corner)
+    left[0:pair, :] = corner
 
     all_of(c_all, 3).wait_recv()
     cols_packed = jnp.concatenate([c_all[j] for j in range(nc)], axis=0)
-    c_full[0:half, :] = jnp.minimum(c_full[0:half, :], cols_packed)
-    c_full[half:rows_here, :] = jnp.minimum(
-        c_full[half:rows_here, :], pltpu.roll(cols_packed, pair, 1))
+    left[pair : pair + half, :] = jnp.minimum(bounds[pair : pair + half, cols_here:], cols_packed)
+    left[pair + half :, :] = jnp.minimum(
+        bounds[pair + half :, cols_here:], pltpu.roll(cols_packed, pair, 1))
 
     def finish(b, carry):
         at = pl.ds(pl.multiple_of(b * PIVOT, PIVOT), PIVOT)
-        out[at, :] = minplus(out[at, :], c_full[at, 0:pair], t_ref)
+        to = pl.ds(pl.multiple_of(pair + b * PIVOT, PIVOT), PIVOT)
+        first = jnp.where(b < pair // PIVOT, 0, pair)
+        factors = left[at, :]
+        total = work[to, :]
+        for k in range(pair):
+            total = jnp.minimum(total, factors[:, k : k + 1] + work[pl.ds(first + k, 1), :])
+        work[to, :] = total
         return carry
 
-    lax.fori_loop(0, rows_here // PIVOT, finish, 0)
+    lax.fori_loop(0, (pair + rows_here) // PIVOT, finish, 0)
+    out[...] = work[2 * pair :, :]
     for kind, buffer in enumerate([c_recv, e_all, r_recv, c_all, k_all]):
         all_of(buffer, kind).wait_send()
 
@@ -268,6 +268,7 @@
     rows_here, cols_here = distances.shape
     half = rows_here // 2
     piece = half // nc
+    pair = 2 * PIVOT
     depth = pl.next_power_of_2(pl.cdiv(NEIGHBORS, cols_here // edge_lengths.shape[1]))
     vmem = pl.BlockSpec(memory_space=pltpu.VMEM)
     f32 = jnp.float32
@@ -285,16 +286,18 @@
             dma((4,)),
             pltpu.VMEM((nr * nc, depth, cols_here), f32),
             pltpu.VMEM((nr * nc, depth, cols_here), f32),
-            pltpu.VMEM((rows_here, NEIGHBORS), jnp.int32),
-            pltpu.VMEM((rows_here, NEIGHBORS), f32),
+            pltpu.VMEM((pair + rows_here, NEIGHBORS), jnp.int32),
+            pltpu.VMEM((pair + rows_here, NEIGHBORS), f32),
             pltpu.VMEM((nc, piece, cols_here), f32),
             pltpu.VMEM((nc, piece, cols_here), f32),
             pltpu.VMEM((nc, piece, cols_here), f32),
-            pltpu.VMEM((rows_here, cols_here), f32),
+            pltpu.VMEM((pair + rows_here, cols_here), f32),
             pltpu.VMEM((nr, 2 * PIVOT, cols_here), f32),
             pltpu.VMEM((nr * nc, 1, cols_here), f32),
-            pltpu.VMEM((2 * PIVOT, cols_here), f32),
-            pltpu.VMEM((2 * PIVOT, cols_here), f32),
+            pltpu.VMEM((pair, cols_here), f32),
+            pltpu.VMEM((2 * pair + rows_here, cols_here), f32),
+            pltpu.VMEM((pair + rows_here, 1), jnp.int32),
+            pltpu.VMEM((pair + rows_here, 2 * cols_here), f32),
             dma((5, 2)),
         ],
         compiler_params=pltpu.CompilerParams(

time: 25.2 us -> 25.3 us (level)
  no operation moved by 1% of the time
where the time goes in v9:
time: 25.3 us; the launch traced here: 25.2 us
  Pallas kernels  24.5 us (97%)
  local copies, waits for them, and re-layouts  0.66 us (3%)
    pallas_call x1, Pallas kernels, on_device(): pl.pallas_call(functools.partial(kernel, nr, nc), out_shape=jax.ShapeDtyp...  24.5 us
    unnamed x1, local copies, waits for them, and re-layouts  0.66 us

profile of v9, /device:TPU:0, one launch (start us, length us, event | category | flops | bytes accessed | tf_op | source)
XLA Modules:
  0.0 25.2 jit_solution(1285333688355264840)
XLA Ops:
  0.0 24.5 %shard_map.46 = f32[256,128]{1,0:T(8,128)S(1)} custom-call(s32[2]{0:T(128)} %pivots_in.1, f32[256,128]{1,0:T(8,128)} %dist_in.1, s32[10,1024]{1,0:T(8,128)} %ids_in.1, f32[10,32]{1,0:T(8,128)} %lens_in.1), custom_call_target="tpu_custom_call" | custom-call | tf_op jit(solution)/shard_map/pallas_call | solution.py:276
  24.5 0.7 %copy.6 = f32[256,128]{1,0:T(8,128)} copy(f32[256,128]{1,0:T(8,128)S(1)} %shard_map.46) | data formatting | bytes 262144

commit v10 on v9

--- a/solution.py
+++ b/solution.py
@@ -56,6 +56,26 @@
     row_peers = [lax.rem(r + i, nr) for i in range(1, nr)]
     col_peers = [lax.rem(c + i, nc) for i in range(1, nc)]
 
+    barrier = pltpu.get_barrier_semaphore()
+
+    def every_peer(act):
+        if devices > 1:
+
+            def step(i, carry):
+                other = lax.rem(me + i, devices)
+                act(lax.div(other, nc), lax.rem(other, nc))
+                return carry
+
+            lax.fori_loop(1, devices, step, 0)
+            return
+        for i in range(nr):
+            for j in range(nc):
+                if i or j:
+                    act(row_peers[i - 1] if i else r, col_peers[j - 1] if j else c)
+
+    every_peer(lambda row, col: pl.semaphore_signal(
+        barrier, inc=1, device_id=(row, col), device_id_type=MESH))
+
     loads = [
         pltpu.make_async_copy(src, dst, in_sem.at[i])
         for i, (src, dst) in enumerate(
@@ -63,27 +83,6 @@
     ]
     for load in loads:
         load.start()
-
-    barrier = pltpu.get_barrier_semaphore()
-
-    def every_peer(act):
-        if devices > 1:
-
-            def step(i, carry):
-                other = lax.rem(me + i, devices)
-                act(lax.div(other, nc), lax.rem(other, nc))
-                return carry
-
-            lax.fori_loop(1, devices, step, 0)
-            return
-        for i in range(nr):
-            for j in range(nc):
-                if i or j:
-                    act(row_peers[i - 1] if i else r, col_peers[j - 1] if j else c)
-
-    every_peer(lambda row, col: pl.semaphore_signal(
-        barrier, inc=1, device_id=(row, col), device_id_type=MESH))
-
     for load in loads:
         load.wait()
     p = [pivots[q] for q in range(2)]
@@ -145,8 +144,6 @@
     c_recv[c] = c_send[c]
     for peer in col_peers:
         send(c_send.at[peer], c_recv.at[c], 0, (r, peer))
-    for peer in row_peers:
-        send(r_recv.at[r], r_recv.at[r], 2, (peer, c))
 
     for t in range(0, rows_here, cols_here):
         start = pl.multiple_of(r * rows_here + t, cols_here)
@@ -183,6 +180,8 @@
     k_all[me] = flat
 
     every_peer(lambda row, col: send(k_all.at[me], k_all.at[me], 4, (row, col)))
+    for peer in row_peers:
+        send(r_recv.at[r], r_recv.at[r], 2, (peer, c))
     all_of(c_recv, 0).wait_recv()
     arrived = [c_recv[j] for j in range(nc)]
     c_all[c] = jnp.where(lane % pair < PIVOT, pick(arrived, col_root[0]), pick(arrived, col_root[1]))
@@ -248,9 +247,9 @@
         bounds[pair + half :, cols_here:], pltpu.roll(cols_packed, pair, 1))
 
     def finish(b, carry):
-        at = pl.ds(pl.multiple_of(b * PIVOT, PIVOT), PIVOT)
-        to = pl.ds(pl.multiple_of(pair + b * PIVOT, PIVOT), PIVOT)
-        first = jnp.where(b < pair // PIVOT, 0, pair)
+        at = pl.ds(pl.multiple_of(b * pair, pair), pair)
+        to = pl.ds(pl.multiple_of(pair + b * pair, pair), pair)
+        first = jnp.minimum(b, 1) * pair
         factors = left[at, :]
         total = work[to, :]
         for k in range(pair):
@@ -258,7 +257,7 @@
         work[to, :] = total
         return carry
 
-    lax.fori_loop(0, (pair + rows_here) // PIVOT, finish, 0)
+    lax.fori_loop(0, (pair + rows_here) // pair, finish, 0)
     out[...] = work[2 * pair :, :]
     for kind, buffer in enumerate([c_recv, e_all, r_recv, c_all, k_all]):
         all_of(buffer, kind).wait_send()

time: 25.3 us -> 24.5 us (0.968)
  Pallas kernels: 24.5 us -> 23.7 us
    pallas_call x1, Pallas kernels: 24.5 us -> 23.7 us  [on_device(): pl.pallas_call(functools.partial(kernel, nr, nc), out_shape=jax.ShapeDtyp...]
where the time goes in v10:
time: 24.5 us; the launch traced here: 24.4 us
  Pallas kernels  23.7 us (97%)
  local copies, waits for them, and re-layouts  0.66 us (3%)
    pallas_call x1, Pallas kernels, on_device(): pl.pallas_call(functools.partial(kernel, nr, nc), out_shape=jax.ShapeDtyp...  23.7 us
    unnamed x1, local copies, waits for them, and re-layouts  0.66 us

profile of v10, /device:TPU:0, one launch (start us, length us, event | category | flops | bytes accessed | tf_op | source)
XLA Modules:
  0.0 24.4 jit_solution(13575736963948486427)
XLA Ops:
  0.0 23.7 %shard_map.46 = f32[256,128]{1,0:T(8,128)S(1)} custom-call(s32[2]{0:T(128)} %pivots_in.1, f32[256,128]{1,0:T(8,128)} %dist_in.1, s32[10,1024]{1,0:T(8,128)} %ids_in.1, f32[10,32]{1,0:T(8,128)} %lens_in.1), custom_call_target="tpu_custom_call" | custom-call | tf_op jit(solution)/shard_map/pallas_call | solution.py:275
  23.7 0.7 %copy.6 = f32[256,128]{1,0:T(8,128)} copy(f32[256,128]{1,0:T(8,128)S(1)} %shard_map.46) | data formatting | bytes 262144

commit v11 on v10

--- a/solution.py
+++ b/solution.py
@@ -182,12 +182,6 @@
     every_peer(lambda row, col: send(k_all.at[me], k_all.at[me], 4, (row, col)))
     for peer in row_peers:
         send(r_recv.at[r], r_recv.at[r], 2, (peer, c))
-    all_of(c_recv, 0).wait_recv()
-    arrived = [c_recv[j] for j in range(nc)]
-    c_all[c] = jnp.where(lane % pair < PIVOT, pick(arrived, col_root[0]), pick(arrived, col_root[1]))
-    for peer in col_peers:
-        send(c_all.at[c], c_all.at[c], 3, (r, peer))
-
     def spread(tiles):
         parts = []
         for g in range(-(-NEIGHBORS // depth)):
@@ -213,7 +207,13 @@
             id_ref[at, :], col_ids, ids_r[at, :], len_r[at, :], ids_cols, len_cols)
         return carry
 
-    lax.fori_loop(0, (pair + rows_here) // PIVOT, bound_rows, 0)
+    lax.fori_loop(0, pair // PIVOT, bound_rows, 0)
+    all_of(c_recv, 0).wait_recv()
+    arrived = [c_recv[j] for j in range(nc)]
+    c_all[c] = jnp.where(lane % pair < PIVOT, pick(arrived, col_root[0]), pick(arrived, col_root[1]))
+    for peer in col_peers:
+        send(c_all.at[c], c_all.at[c], 3, (r, peer))
+    lax.fori_loop(pair // PIVOT, (pair + rows_here) // PIVOT, bound_rows, 0)
 
     all_of(r_recv, 2).wait_recv()
     rows_panel = jnp.concatenate(
@@ -240,12 +240,6 @@
     corner = lax.fori_loop(0, 6, lambda _, a: square(a, k_ref.at[0:PIVOT, :]), corner)
     left[0:pair, :] = corner
 
-    all_of(c_all, 3).wait_recv()
-    cols_packed = jnp.concatenate([c_all[j] for j in range(nc)], axis=0)
-    left[pair : pair + half, :] = jnp.minimum(bounds[pair : pair + half, cols_here:], cols_packed)
-    left[pair + half :, :] = jnp.minimum(
-        bounds[pair + half :, cols_here:], pltpu.roll(cols_packed, pair, 1))
-
     def finish(b, carry):
         at = pl.ds(pl.multiple_of(b * pair, pair), pair)
         to = pl.ds(pl.multiple_of(pair + b * pair, pair), pair)
@@ -257,7 +251,13 @@
         work[to, :] = total
         return carry
 
-    lax.fori_loop(0, (pair + rows_here) // pair, finish, 0)
+    lax.fori_loop(0, 1, finish, 0)
+    all_of(c_all, 3).wait_recv()
+    cols_packed = jnp.concatenate([c_all[j] for j in range(nc)], axis=0)
+    left[pair : pair + half, :] = jnp.minimum(bounds[pair : pair + half, cols_here:], cols_packed)
+    left[pair + half :, :] = jnp.minimum(
+        bounds[pair + half :, cols_here:], pltpu.roll(cols_packed, pair, 1))
+    lax.fori_loop(1, (pair + rows_here) // pair, finish, 0)
     out[...] = work[2 * pair :, :]
     for kind, buffer in enumerate([c_recv, e_all, r_recv, c_all, k_all]):
         all_of(buffer, kind).wait_send()

time: 24.5 us -> 24.5 us (level)
  no operation moved by 1% of the time
where the time goes in v11:
time: 24.5 us; the launch traced here: 24.3 us
  Pallas kernels  23.7 us (97%)
  local copies, waits for them, and re-layouts  0.66 us (3%)
    pallas_call x1, Pallas kernels, on_device(): pl.pallas_call(functools.partial(kernel, nr, nc), out_shape=jax.ShapeDtyp...  23.7 us
    unnamed x1, local copies, waits for them, and re-layouts  0.66 us

profile of v11, /device:TPU:0, one launch (start us, length us, event | category | flops | bytes accessed | tf_op | source)
XLA Modules:
  0.0 24.3 jit_solution(9506786361709965093)
XLA Ops:
  0.0 23.7 %shard_map.46 = f32[256,128]{1,0:T(8,128)S(1)} custom-call(s32[2]{0:T(128)} %pivots_in.1, f32[256,128]{1,0:T(8,128)} %dist_in.1, s32[10,1024]{1,0:T(8,128)} %ids_in.1, f32[10,32]{1,0:T(8,128)} %lens_in.1), custom_call_target="tpu_custom_call" | custom-call | tf_op jit(solution)/shard_map/pallas_call | solution.py:275
  23.7 0.7 %copy.6 = f32[256,128]{1,0:T(8,128)} copy(f32[256,128]{1,0:T(8,128)S(1)} %shard_map.46) | data formatting | bytes 262144
